TPU v7x, 32 devices: a whole 2x2x4 slice. The times are simulated.
32 devices in a mesh: dp: 16 (over z, y, core), slab: 2 (over x).
Axes of the slice: x: 2, y: 2, z: 4, core: 2. Of those that a mesh axis runs over, the one named last changes fastest.
Arguments:
- snapshots: bfloat16 [16, 64, 512, 512], P('dp', None, 'slab'), may hold values from -6 to 6
- cotangent: bfloat16 [16, 64, 512, 512], P('dp', None, 'slab'), may hold values from -6 to 6
- w_spec: float32 [32, 32, 64, 128], P('slab', 'dp'), may hold values from -0.5 to 0.5
- first_moment: float32 [32, 32, 64, 128], P('slab', 'dp'), may hold values from -6 to 6
- second_moment: float32 [32, 32, 64, 128], P('slab', 'dp'), may hold values from 0.1 to 4
- w_skip: bfloat16 [64, 64], replicated, may hold values from -0.75 to 0.75
- bias: float32 [64], replicated, may hold values from -3 to 3
Outputs:
- layer_out: bfloat16 [16, 64, 512, 512], P('dp', None, 'slab')
- new_weights: float32 [32, 32, 64, 128], P('slab', 'dp')
- new_first: float32 [32, 32, 64, 128], P('slab', 'dp')
- new_second: float32 [32, 32, 64, 128], P('slab', 'dp')
All inputs are finite; a program needn't handle non-finite values.
Results may differ from a plain program's by a relative error of at most 0.001.
Values sent between devices are 32-bit elements; how exact they have to be, the bound alone decides.
A program may use at most 192 MiB of HBM per device.

v0:
```python
import math
import jax
import jax.numpy as jnp
from jax import lax
from jax.sharding import PartitionSpec as P

NY = 512
NZ = 512
KY = 32
KZ = 32
high = lax.Precision.HIGHEST
gelu_coef = 0.7978845608028654
cube_coef = 0.044715


def gelu_value(x):
    return 0.5 * x * (1.0 + jnp.tanh(gelu_coef * (x + cube_coef * x * x * x)))


def gelu_slope(x):
    tanh_val = jnp.tanh(gelu_coef * (x + cube_coef * x * x * x))
    return 0.5 * (1.0 + tanh_val) + 0.5 * x * (1.0 - tanh_val * tanh_val) * gelu_coef * (
        1.0 + 3.0 * cube_coef * x * x
    )


def z_tables(length):
    zpos = jnp.arange(length, dtype=jnp.int32)[:, None]
    kpos = jnp.arange(KZ, dtype=jnp.int32)[None, :]
    angle = 2.0 * math.pi / length * jnp.remainder(zpos * kpos, length).astype(jnp.float32)
    return (jnp.cos(angle), jnp.sin(angle))


def y_tables(count):
    half = KY // 2
    freq = jnp.concatenate(
        [jnp.arange(half, dtype=jnp.int32), jnp.arange(half, dtype=jnp.int32) - half]
    )
    ypos = jnp.arange(count, dtype=jnp.int32)
    phase = jnp.remainder(ypos[:, None] * freq[None, :], NY)
    angle = 2.0 * math.pi / NY * phase.astype(jnp.float32)
    return (jnp.cos(angle), jnp.sin(angle))


def y_forward(flat, ycos, ysin, count):
    with_cos = jnp.einsum("cyk,yj->ckj", flat, ycos, precision=high)
    with_sin = jnp.einsum("cyk,yj->ckj", flat, ysin, precision=high)
    real_part = with_cos[:, :count] + with_sin[:, count:]
    imag_part = with_cos[:, count:] - with_sin[:, :count]
    return jnp.stack([real_part, imag_part], 0).transpose(2, 0, 1, 3)


def y_inverse(spec, ycos, ysin):
    vreal = spec[:, 0]
    vimag = spec[:, 1]
    yreal = jnp.einsum("koj,yj->oyk", vreal, ycos, precision=high) - jnp.einsum(
        "koj,yj->oyk", vimag, ysin, precision=high
    )
    yimag = jnp.einsum("koj,yj->oyk", vreal, ysin, precision=high) + jnp.einsum(
        "koj,yj->oyk", vimag, ycos, precision=high
    )
    return (yreal, yimag)


def forward_modes(field):
    chans, rows, length = field.shape
    zcos, zsin = z_tables(length)
    table = jnp.concatenate([zcos, -zsin], axis=1)
    along_z = jnp.dot(
        field.reshape(chans * rows, length),
        table,
        precision=high,
        preferred_element_type=jnp.float32,
    )
    along_z = along_z.reshape(chans, rows, 2, KZ)
    pencil = lax.all_to_all(along_z, "slab", split_axis=3, concat_axis=1, tiled=True)
    local_modes = pencil.shape[3]
    ycos, ysin = y_tables(NY)
    return y_forward(pencil.reshape(chans, NY, 2 * local_modes), ycos, ysin, local_modes)


def inverse_modes(spec, rows, length):
    chans = spec.shape[2]
    zcos, zsin = z_tables(length)
    ycos, ysin = y_tables(NY)
    yreal, yimag = y_inverse(spec, ycos, ysin)
    both = jnp.stack([yreal, yimag], 2)
    slabs = lax.all_to_all(both, "slab", split_axis=1, concat_axis=3, tiled=True)
    back_table = jnp.concatenate([zcos.T, -zsin.T], axis=0)
    total = jnp.dot(
        slabs.reshape(chans * rows, 2 * KZ),
        back_table,
        precision=high,
        preferred_element_type=jnp.float32,
    )
    return total.reshape(chans, rows, length)


def body(snapshots, cotangent, w_spec, first_moment, second_moment, w_skip, bias):
    chans, rows, length = snapshots.shape[1:]
    spec_scale = 1.0 / math.sqrt(NY * NZ)
    out_scale = 1.0 / math.sqrt(KY * KZ)
    count = lax.axis_size("dp")
    field_low = snapshots[0]
    weights = lax.all_gather(w_spec, "dp", axis=1, tiled=True)
    spec_u = forward_modes(field_low.astype(jnp.float32)) * spec_scale
    ureal = spec_u[:, 0]
    uimag = spec_u[:, 1]
    first_part = jnp.einsum("kij,kjio->koj", ureal, weights, precision=high)
    second_part = jnp.einsum("kij,kjio->koj", uimag, weights, precision=high)
    vreal = first_part[:, :chans] - second_part[:, chans:]
    vimag = first_part[:, chans:] + second_part[:, :chans]
    spec_v = jnp.stack([vreal, vimag], 1)
    mixed = inverse_modes(spec_v, rows, length) * out_scale
    skip = jnp.einsum(
        "io,in->on",
        w_skip,
        field_low.reshape(chans, rows * length),
        preferred_element_type=jnp.float32,
    )
    pre = mixed + skip.reshape(chans, rows, length) + bias[:, None, None]
    layer_out = gelu_value(pre).astype(jnp.bfloat16)[None]
    slope = cotangent[0].astype(jnp.float32) * gelu_slope(pre)
    spec_g = forward_modes(slope) * out_scale
    greal = spec_g[:, 0]
    gimag = spec_g[:, 1]
    grad_real = jnp.einsum("kij,koj->kjio", ureal, greal, precision=high) + jnp.einsum(
        "kij,koj->kjio", uimag, gimag, precision=high
    )
    grad_imag = jnp.einsum("kij,koj->kjio", ureal, gimag, precision=high) - jnp.einsum(
        "kij,koj->kjio", uimag, greal, precision=high
    )
    summed = lax.psum_scatter(
        jnp.concatenate([grad_real, grad_imag], axis=-1), "dp", scatter_dimension=1, tiled=True
    )
    grad = summed / count
    new_first = 0.9 * first_moment + 0.1 * grad
    new_second = 0.95 * second_moment + 0.05 * grad * grad
    bias_first = 1.0 - 0.9**10
    bias_second = 1.0 - 0.95**10
    new_weights = w_spec - 0.01 * (new_first / bias_first) / (
        jnp.sqrt(new_second / bias_second) + 1e-08
    )
    return (layer_out, new_weights, new_first, new_second)


def solution(mesh):
    placed = (
        P("dp", None, "slab", None),
        P("dp", None, "slab", None),
        P("slab", "dp", None, None),
        P("slab", "dp", None, None),
        P("slab", "dp", None, None),
        P(),
        P(),
    )
    return jax.shard_map(
        body,
        mesh=mesh,
        in_specs=placed,
        out_specs=(
            P("dp", None, "slab", None),
            P("slab", "dp", None, None),
            P("slab", "dp", None, None),
            P("slab", "dp", None, None),
        ),
        check_vma=False,
    )
```

profile of v0, /device:TPU:0, one launch (start us, length us, event | category | flops | bytes accessed | tf_op | source)
XLA Modules:
  0.0 820.8 jit_solution(16519467777478254915)
XLA Ops:
  7.2 0.7 all-gather.2.cloned.1.call-update
  7.9 0.3 sine_negate_fusion.1
  8.2 18.1 %fusion.120 = f32[64,16384]{1,0:T(8,128)S(1)} fusion(bf16[16384,512]{1,0:T(8,128)(2,1)} %bitcast.145, f32[512,32]{0,1:T(8,128)S(1)} %get-tuple-element.19, f32[512,32]{0,1:T(8,128)S(1)} %get-tuple-element.20), kind=kOutput, calls=%fused_computation.154 | convolution fusion | flops 6442483712 | bytes 21102592 | tf_op jit(solution)/shard_map/dot_general | solution.py:69
  26.3 1.3 copy.53
  27.6 2.3 copy.30
  29.9 5.6 all-to-all-start
  35.6 48.7 %all-to-all-done = f32[64,256,2,32]{1,0,2,3:T(8,128)} async-done(((f32[64,256,2,32]{1,0,2,3:T(8,128)}), f32[64,256,2,32]{1,0,2,3:T(8,128)}, u32[]{:S(2)}, u32[]{:S(2)}) %all-to-all-start) | async-done | bytes 4194336 | tf_op jit(solution)/shard_map/all_to_all | solution.py:76
  84.4 7.4 copy.68
  91.8 6.6 reshape.41
  98.4 6.1 fusion.52
  104.5 6.1 fusion.58
  111.1 0.2 copy.43
  111.6 28.3 %all-gather.2.cloned.1.call-done = f32[16,32,64,128]{3,2,1,0:T(8,128)} async-done(((f32[16,2,64,128]{3,2,1,0:T(8,128)}), f32[16,32,64,128]{3,2,1,0:T(8,128)}) %all-gather.2.cloned.1.call-update) | async-done | bytes 16777232 | tf_op jit(solution)/shard_map/all_gather | solution.py:105
  139.9 17.5 %fusion.121 = f32[16,32,1,128]{3,2,1,0:T(1,128)S(1)} fusion(f32[16,64,32,1]{1,3,2,0:T(1,128)S(1)} %copy.43, f32[16,32,64,128]{3,2,1,0:T(8,128)} %all-gather.2.cloned.1.call-done), kind=kOutput, calls=%fused_computation.156 | convolution fusion | flops 50331648 | bytes 17170432 | tf_op jit(solution)/shard_map/kij,kjio->koj/dot_general | solution.py:109
  157.3 15.1 %fusion.122 = f32[16,32,1,128]{3,2,1,0:T(1,128)S(1)} fusion(f32[16,64,32,1]{1,3,2,0:T(1,128)S(1)} %copy.45, f32[16,32,64,128]{3,2,1,0:T(8,128)S(1)} %copy-done.2), kind=kOutput, calls=%fused_computation.157 | convolution fusion | flops 50331648 | bytes 17170432 | tf_op jit(solution)/shard_map/kij,kjio->koj/dot_general | solution.py:110
  172.4 2.3 fusion.37
  174.7 2.3 fusion.38
  177.0 2.3 add_bitcast_fusion
  179.3 2.3 subtract_bitcast_fusion
  181.6 2.5 pad_maximum_fusion.1
  184.1 9.1 %copy.32 = f32[64,512,2,16]{0,3,2,1:T(8,128)} copy(f32[64,512,2,16]{1,0,3,2:T(8,128)} %pad_maximum_fusion.1) | data formatting | bytes 8388608 | tf_op jit(solution)/shard_map/stack | solution.py:87
  193.2 8.7 %reshape.57 = f32[2,1,524288]{2,1,0:T(1,128)} reshape(f32[512,2,16,64]{3,2,1,0:T(8,128)} %bitcast.147) | data formatting | bytes 8388608
  201.9 5.6 all-to-all-start.1
  207.6 0.3 sine_negate_fusion
  207.8 35.3 %fusion.19 = f32[64,256,512]{2,0,1:T(8,128)} fusion(bf16[64,64]{1,0:T(8,128)(2,1)S(1)} %copy-done, bf16[8,8,256,512]{3,2,1,0:T(8,128)(2,1)} %bitcast.146), kind=kOutput, calls=%fused_computation.21 | convolution fusion | flops 1073741824 | bytes 50339840 | tf_op jit(solution)/shard_map/io,in->on/dot_general | solution.py:115
  243.1 12.5 %all-to-all-done.1 = f32[2,1,524288]{2,1,0:T(1,128)} async-done(((f32[2,1,524288]{2,1,0:T(1,128)}), f32[2,1,524288]{2,1,0:T(1,128)}, u32[]{:S(2)}, u32[]{:S(2)}) %all-to-all-start.1) | async-done | bytes 4194336 | tf_op jit(solution)/shard_map/all_to_all | solution.py:88
  255.6 0.5 broadcast.184
  256.1 16.5 %reduce = f32[2,524288]{1,0:T(2,128)} reduce(f32[2,1,524288]{2,1,0:T(1,128)} %all-to-all-done.1, f32[]{:T(128)} %broadcast.184), dimensions={1}, to_apply=%all_to_all.36.reduce_sub_computation | reduce | bytes 8388612 | tf_op jit(solution)/shard_map/all_to_all | solution.py:88
  272.7 10.1 %reshape.58 = f32[512,2,16,64]{3,2,1,0:T(8,128)} reshape(f32[2,524288]{1,0:T(2,128)} %reduce) | data formatting | bytes 8388608
  282.8 8.7 %copy.33 = f32[64,2,256,2,16]{2,4,1,3,0:T(8,128)} copy(f32[64,2,256,2,16]{0,4,3,2,1:T(8,128)} %bitcast.148) | data formatting | bytes 8388608 | tf_op jit(solution)/shard_map/all_to_all | solution.py:88
  291.5 56.3 %fusion.10 = f32[64,256,512]{2,1,0:T(8,128)} fusion(f32[64,256,512]{2,0,1:T(8,128)} %fusion.19, f32[64]{0:T(128)S(1)} %copy-done.6, f32[64,256,64]{1,2,0:T(8,128)} %bitcast.149, f32[32,512]{1,0:T(8,128)S(1)} %get-tuple-element.21, f32[32,512]{1,0:T(8,128)S(1)} %get-tuple-element.22), kind=kOutput, calls=%fused_computation.12 | convolution fusion | flops 6467649536 | bytes 71434496 | tf_op jit(solution)/shard_map/dot_general | solution.py:90
  347.8 57.3 %fusion.7 = f32[64,256,2,32]{1,3,2,0:T(8,128)S(1)} fusion(f32[2,32,512,1]{2,1,0,3:T(8,128)S(1)} %bitcast.162, f32[64,256,512]{2,1,0:T(8,128)} %fusion.10, bf16[1,64,256,512]{3,2,1,0:T(8,128)(2,1)} %param.8), kind=kOutput, calls=%fused_computation.9 | convolution fusion | flops 6601834496 | bytes 54657024 | tf_op jit(solution)/shard_map/dot_general | solution.py:69
  405.1 5.2 copy.38
  410.3 5.6 all-to-all-start.2
  415.9 0.2 copy.37
  416.4 46.7 %all-to-all-done.2 = f32[64,256,2,32]{1,2,0,3:T(2,128)} async-done(((f32[64,256,2,32]{1,2,0,3:T(2,128)}), f32[64,256,2,32]{1,2,0,3:T(2,128)}, u32[]{:S(2)}, u32[]{:S(2)}) %all-to-all-start.2) | async-done | bytes 4194336 | tf_op jit(solution)/shard_map/all_to_all | solution.py:76
  463.2 7.4 copy.67
  470.6 6.7 reshape.42
  477.3 6.1 fusion.48
  483.4 6.1 fusion.54
  489.9 0.2 copy.40
  490.4 11.3 %multiply_add_fusion.1 = (f32[16,32,64,64]{3,2,1,0:T(8,128)S(1)}, f32[16,32,64,64]{3,2,1,0:T(8,128)}) fusion(f32[16,32,64]{2,1,0:T(8,128)S(1)} %copy.42, f32[16,32,64]{2,1,0:T(8,128)S(1)} %copy.41, f32[16,32,64]{2,1,0:T(8,128)S(1)} %copy.40, f32[16,32,64]{2,1,0:T(8,128)S(1)} %copy.37), kind=kLoop, calls=%fused_computation.27 | loop fusion | flops 12582912 | bytes 17301504 | tf_op jit(solution)/shard_map/add | solution.py:127
  501.6 13.1 %pad_maximum_fusion = f32[16,32,64,128]{3,2,1,0:T(8,128)} fusion(f32[16,32,64,64]{3,2,1,0:T(8,128)} %get-tuple-element.12, f32[16,32,64,64]{3,2,1,0:T(8,128)S(1)} %get-tuple-element.11), kind=kLoop, calls=%fused_computation.24 | loop fusion | flops 4194304 | bytes 33554432 | tf_op jit(solution)/shard_map/concatenate | solution.py:134
  514.8 0.6 copy-done.7
  515.4 0.6 dynamic-slice
  516.7 22.3 %fusion.28 = bf16[1,64,256,512]{3,2,1,0:T(8,128)(2,1)} fusion(f32[64,256,512]{2,1,0:T(8,128)} %fusion.10), kind=kLoop, calls=%fused_computation.33 | loop fusion | flops 75497472 | bytes 50331648 | tf_op jit(solution)/shard_map/broadcast_in_dim | solution.py:122
  539.0 271.4 %all-reduce.3.cloned.1.call-done = f32[16,32,64,128]{3,2,1,0:T(8,128)} async-done(((f32[16,32,64,128]{3,2,1,0:T(8,128)}), f32[16,32,64,128]{3,2,1,0:T(8,128)}) %all-reduce.3.cloned.1.call-update) | async-done | bytes 16777232
  810.4 3.3 divide_subtract_fusion
  (31 shorter events, 1.7 us)
Async XLA Ops:
  7.2 200.7 %copy-start = (bf16[64,64]{1,0:T(8,128)(2,1)S(1)}, bf16[64,64]{1,0:T(8,128)(2,1)}, u32[]{:S(2)}) copy-start(bf16[64,64]{1,0:T(8,128)(2,1)} %param.12) | copy-start | bytes 24580
  7.2 132.7 %all-gather.2.cloned.1.call-start = ((), (), s32[]{:S(2)}) async-start(), calls=%async_computation.3 | async-start | bytes 17825792 | tf_op jit(solution)/shard_map/all_gather | solution.py:105
  29.9 54.5 %all-to-all-start = ((f32[64,256,2,32]{1,0,2,3:T(8,128)}), f32[64,256,2,32]{1,0,2,3:T(8,128)}, u32[]{:S(2)}, u32[]{:S(2)}) async-start(f32[64,256,2,32]{1,0,2,3:T(8,128)} %copy.30), calls=%async_computation | async-start | bytes 8388608 | tf_op jit(solution)/shard_map/all_to_all | solution.py:76
  139.9 17.5 %copy-start.2 = (f32[16,32,64,128]{3,2,1,0:T(8,128)S(1)}, f32[16,32,64,128]{3,2,1,0:T(8,128)}, u32[]{:S(2)}) copy-start(f32[16,32,64,128]{3,2,1,0:T(8,128)} %all-gather.2.cloned.1.call-done) | copy-start | bytes 50331652
  201.9 53.7 %all-to-all-start.1 = ((f32[2,1,524288]{2,1,0:T(1,128)}), f32[2,1,524288]{2,1,0:T(1,128)}, u32[]{:S(2)}, u32[]{:S(2)}) async-start(f32[2,1,524288]{2,1,0:T(1,128)} %reshape.57), calls=%async_computation.1 | async-start | bytes 8388608 | tf_op jit(solution)/shard_map/all_to_all | solution.py:88
  256.1 35.4 %copy-start.6 = (f32[64]{0:T(128)S(1)}, f32[64]{0:T(128)}, u32[]{:S(2)}) copy-start(f32[64]{0:T(128)} %param.13) | copy-start | bytes 772
  410.3 52.8 %all-to-all-start.2 = ((f32[64,256,2,32]{1,2,0,3:T(2,128)}), f32[64,256,2,32]{1,2,0,3:T(2,128)}, u32[]{:S(2)}, u32[]{:S(2)}) async-start(f32[64,256,2,32]{1,2,0,3:T(2,128)} %copy.38), calls=%async_computation.2 | async-start | bytes 8388608 | tf_op jit(solution)/shard_map/all_to_all | solution.py:76
  415.9 394.5 %all-reduce.3.cloned.1.call-start = ((), (), s32[]{:S(2)}) async-start(), calls=%async_computation.4 | async-start | bytes 33554432
  514.7 0.7 copy-start.7
  516.0 297.8 %copy-start.1 = (bf16[64,64]{1,0:T(8,128)(2,1)S(1)}, bf16[64,64]{1,0:T(8,128)(2,1)}, u32[]{:S(2)}) copy-start(bf16[64,64]{1,0:T(8,128)(2,1)} %param.12) | copy-start | bytes 24580
  516.6 293.8 %copy-start.3 = (f32[16,2,64,128]{3,2,1,0:T(8,128)S(1)}, f32[16,2,64,128]{3,2,1,0:T(8,128)}, u32[]{:S(2)}) copy-start(f32[16,2,64,128]{3,2,1,0:T(8,128)} %param.9) | copy-start | bytes 3145732
  516.7 293.8 %copy-start.4 = (f32[16,2,64,128]{3,2,1,0:T(8,128)S(1)}, f32[16,2,64,128]{3,2,1,0:T(8,128)}, u32[]{:S(2)}) copy-start(f32[16,2,64,128]{3,2,1,0:T(8,128)} %param.10) | copy-start | bytes 3145732
  516.7 293.8 %copy-start.5 = (f32[16,2,64,128]{3,2,1,0:T(8,128)S(1)}, f32[16,2,64,128]{3,2,1,0:T(8,128)}, u32[]{:S(2)}) copy-start(f32[16,2,64,128]{3,2,1,0:T(8,128)} %param.11) | copy-start | bytes 3145732
Sparse Core Ops, SparseCore 0:
  10.2 129.6 all-gather.1
  514.9 295.4 all-reduce.2
where the time goes:
time: 828 us; the launch traced here: 821 us
  waiting for transfers between devices  408 us (49%)
  matrix products  233 us (28%)
  local copies, waits for them, and re-layouts  77.1 us (9%)
  other arithmetic  70.2 us (8%)
  starting transfers between devices  16.8 us (2%)
  between operations  15.2 us (2%)
    unnamed x3, waiting for transfers between devices  272 us
    all_to_all x2, waiting for transfers between devices, forward_modes(): lax.all_to_all(along_z, 'slab', split_axis=3, concat_axis=1, tiled=True)  95.5 us
    dot_general x2, matrix products, forward_modes(): jnp.dot(field.reshape(chans * rows, length), table, precision=high, prefe...  75.4 us
    dot_general x1, matrix products, inverse_modes(): jnp.dot(slabs.reshape(chans * rows, 2 * KZ), back_table, precision=high,...  56.3 us
    dot_general x1, matrix products, body(): jnp.einsum('io,in->on', w_skip, field_low.reshape(chans, rows * length),...  35.3 us
    all_gather x1, waiting for transfers between devices, body(): weights = lax.all_gather(w_spec, 'dp', axis=1, tiled=True)  28.3 us
    broadcast_in_dim x1, other arithmetic, body(): layer_out = gelu_value(pre).astype(jnp.bfloat16)[None]  22.3 us
    unnamed x20, local copies, waits for them, and re-layouts  21.4 us
  transfers between devices with their start and end apart: 5, of which 5 were waited for; matrix products, arithmetic and copies ran while one was open for 13% of the time, Pallas kernels for 0%

commit v1 on v0

--- a/solution.py
+++ b/solution.py
@@ -102,7 +102,23 @@
     out_scale = 1.0 / math.sqrt(KY * KZ)
     count = lax.axis_size("dp")
     field_low = snapshots[0]
-    weights = lax.all_gather(w_spec, "dp", axis=1, tiled=True)
+    devices, index, extent = (lax.axis_size("dp"), lax.axis_index("dp"), w_spec.shape[1])
+    right = [(i, (i + 1) % devices) for i in range(devices)]
+    left = [(i, (i - 1) % devices) for i in range(devices)]
+    weights = jnp.zeros((*w_spec.shape[:1], devices * extent, *w_spec.shape[1 + 1 :]), w_spec.dtype)
+    weights = lax.dynamic_update_slice_in_dim(weights, w_spec, index * extent, axis=1)
+    from_left = from_right = w_spec
+    halfway = devices // 2
+    for step in range(1, halfway + 1):
+        from_left = lax.ppermute(from_left, "dp", right)
+        weights = lax.dynamic_update_slice_in_dim(
+            weights, from_left, (index - step) % devices * extent, axis=1
+        )
+        if step < devices - halfway:
+            from_right = lax.ppermute(from_right, "dp", left)
+            weights = lax.dynamic_update_slice_in_dim(
+                weights, from_right, (index + step) % devices * extent, axis=1
+            )
     spec_u = forward_modes(field_low.astype(jnp.float32)) * spec_scale
     ureal = spec_u[:, 0]
     uimag = spec_u[:, 1]

time: 828 us -> 929 us (1.12)
  starting transfers between devices: 16.8 us -> 118 us
  waiting for transfers between devices: 408 us -> 369 us
  local copies, waits for them, and re-layouts: 77.1 us -> 114 us
    ppermute x0 -> x15, starting transfers between devices: none -> 101 us  [the longest x8 86.1 us: body(): from_left = lax.ppermute(from_left, 'dp', right)]
    all_to_all x2, waiting for transfers between devices: 95.5 us -> 56.4 us  [forward_modes(): lax.all_to_all(along_z, 'slab', split_axis=3, concat_axis=1, tiled=True)]
    ppermute x0 -> x15, waiting for transfers between devices: none -> 29.1 us  [the longest x8 25 us: body(): from_left = lax.ppermute(from_left, 'dp', right)]
    all_gather x1 -> x0, waiting for transfers between devices: 28.3 us -> none  [body(): weights = lax.all_gather(w_spec, 'dp', axis=1, tiled=True)]
    dynamic_update_slice x0 -> x16, local copies, waits for them, and re-layouts: none -> 28.1 us  [the longest x7 13.6 us: body(): lax.dynamic_update_slice_in_dim(weights, from_right, (index + step) % dev...]
    unnamed x3 -> x2, waiting for transfers between devices: 272 us -> 272 us
    unnamed x20 -> x36, local copies, waits for them, and re-layouts: 21.4 us -> 21.4 us
  transfers between devices with their start and end apart: 5 -> 19, of which waited for: 5 -> 9; matrix products, arithmetic and copies ran while one was open for 13% -> 16% of each run, Pallas kernels for 0% -> 0%
where the time goes in v1:
time: 929 us; the launch traced here: 922 us
  waiting for transfers between devices  369 us (40%)
  matrix products  235 us (25%)
  starting transfers between devices  118 us (13%)
  local copies, waits for them, and re-layouts  114 us (12%)
  other arithmetic  70.2 us (8%)
  between operations  15.5 us (2%)
    unnamed x2, waiting for transfers between devices  272 us
    ppermute x8, starting transfers between devices, body(): from_left = lax.ppermute(from_left, 'dp', right)  86.1 us
    dot_general x2, matrix products, forward_modes(): jnp.dot(field.reshape(chans * rows, length), table, precision=high, prefe...  75.4 us
    all_to_all x2, waiting for transfers between devices, forward_modes(): lax.all_to_all(along_z, 'slab', split_axis=3, concat_axis=1, tiled=True)  56.4 us
    dot_general x1, matrix products, inverse_modes(): jnp.dot(slabs.reshape(chans * rows, 2 * KZ), back_table, precision=high,...  56.1 us
    dot_general x1, matrix products, body(): jnp.einsum('io,in->on', w_skip, field_low.reshape(chans, rows * length),...  35.5 us
    ppermute x8, waiting for transfers between devices, body(): from_left = lax.ppermute(from_left, 'dp', right)  25 us
    broadcast_in_dim x1, other arithmetic, body(): layer_out = gelu_value(pre).astype(jnp.bfloat16)[None]  22.2 us
  transfers between devices with their start and end apart: 19, of which 9 were waited for; matrix products, arithmetic and copies ran while one was open for 16% of the time, Pallas kernels for 0%

profile of v1, /device:TPU:0, one launch (start us, length us, event | category | flops | bytes accessed | tf_op | source)
XLA Modules:
  0.0 921.6 jit_solution(17835753755988802782)
XLA Ops:
  7.7 5.1 collective-permute-start.1
  12.7 12.7 %collective-permute-done = f32[16,2,64,128]{3,2,1,0:T(8,128)S(1)} collective-permute-done((f32[16,2,64,128]{3,2,1,0:T(8,128)}, f32[16,2,64,128]{3,2,1,0:T(8,128)S(1)}, u32[]{:S(2)}, u32[]{:S(2)}) %collective-permute-start) | collective-permute-done | bytes 1048608 | tf_op jit(solution)/shard_map/ppermute | solution.py:113
  25.5 8.1 collective-permute-start.2
  33.6 8.9 collective-permute-done.2
  42.5 15.8 %collective-permute-start.4 = (f32[16,2,64,128]{3,2,1,0:T(8,128)S(1)}, f32[16,2,64,128]{3,2,1,0:T(8,128)}, u32[]{:S(2)}, u32[]{:S(2)}) collective-permute-start(f32[16,2,64,128]{3,2,1,0:T(8,128)S(1)} %collective-permute-done.2), channel_id=1, source_target_pairs={{0,2},{2,4},{4,6},{6,8},{8,10},{10,12},{12,14},{14,16},{16,18},{18... | collective-permute-start | bytes 3145736 | tf_op jit(solution)/shard_map/ppermute | solution.py:113
  58.7 3.3 collective-permute-done.4
  62.0 21.6 %collective-permute-start.6 = (f32[16,2,64,128]{3,2,1,0:T(8,128)}, f32[16,2,64,128]{3,2,1,0:T(8,128)S(1)}, u32[]{:S(2)}, u32[]{:S(2)}) collective-permute-start(f32[16,2,64,128]{3,2,1,0:T(8,128)} %collective-permute-done.4), channel_id=1, source_target_pairs={{0,2},{2,4},{4,6},{6,8},{8,10},{10,12},{12,14},{14,16},{16,18},{18... | collective-permute-start | bytes 3145736 | tf_op jit(solution)/shard_map/ppermute | solution.py:113
  83.6 18.1 %fusion.120 = f32[64,16384]{1,0:T(8,128)S(1)} fusion(bf16[16384,512]{1,0:T(8,128)(2,1)} %bitcast.145, f32[512,32]{0,1:T(8,128)S(1)} %get-tuple-element.19, f32[512,32]{0,1:T(8,128)S(1)} %get-tuple-element.20), kind=kOutput, calls=%fused_computation.170 | convolution fusion | flops 6442483712 | bytes 21102592 | tf_op jit(solution)/shard_map/dot_general | solution.py:69
  103.0 2.3 copy.30
  105.3 5.6 all-to-all-start
  111.0 2.6 collective-permute-start.8
  113.7 8.3 broadcast_in_dim.4
  123.6 4.7 collective-permute-start.9
  128.3 19.0 %collective-permute-start.10 = (f32[16,2,64,128]{3,2,1,0:T(8,128)}, f32[16,2,64,128]{3,2,1,0:T(8,128)}, u32[]{:S(2)}, u32[]{:S(2)}) collective-permute-start(f32[16,2,64,128]{3,2,1,0:T(8,128)} %collective-permute-done.8), channel_id=1, source_target_pairs={{0,2},{2,4},{4,6},{6,8},{8,10},{10,12},{12,14},{14,16},{16,18},{18... | collective-permute-start | bytes 3145736 | tf_op jit(solution)/shard_map/ppermute | solution.py:113
  149.5 8.5 all-to-all-done
  158.0 7.5 copy.68
  165.5 6.4 reshape.41
  171.9 6.1 fusion.52
  178.1 6.1 fusion.58
  193.4 3.5 collective-permute-done.11
  196.9 4.7 collective-permute-start.13
  204.0 17.0 %collective-permute-start.14 = (f32[16,2,64,128]{3,2,1,0:T(8,128)}, f32[16,2,64,128]{3,2,1,0:T(8,128)S(1)}, u32[]{:S(2)}, u32[]{:S(2)}) collective-permute-start(f32[16,2,64,128]{3,2,1,0:T(8,128)} %collective-permute-done.12), channel_id=1, source_target_pairs={{0,2},{2,4},{4,6},{6,8},{8,10},{10,12},{12,14},{14,16},{16,18},{18... | collective-permute-start | bytes 3145736 | tf_op jit(solution)/shard_map/ppermute | solution.py:113
  226.6 2.3 constant_dynamic-update-slice_fusion.5
  237.9 16.8 %fusion.122 = f32[16,32,1,128]{3,2,1,0:T(1,128)S(1)} fusion(f32[16,32,64,128]{3,2,1,0:T(8,128)} %constant_dynamic-update-slice_fusion, f32[16,64,32,1]{1,3,2,0:T(1,128)S(1)} %copy.45), kind=kOutput, calls=%fused_computation.173 | convolution fusion | flops 50331648 | bytes 17170432 | tf_op jit(solution)/shard_map/kij,kjio->koj/dot_general | solution.py:126
  254.8 17.0 %fusion.121 = f32[16,32,1,128]{3,2,1,0:T(1,128)S(1)} fusion(f32[16,32,64,128]{3,2,1,0:T(8,128)} %constant_dynamic-update-slice_fusion, f32[16,64,32,1]{1,3,2,0:T(1,128)S(1)} %copy.43), kind=kOutput, calls=%fused_computation.172 | convolution fusion | flops 50331648 | bytes 17170432 | tf_op jit(solution)/shard_map/kij,kjio->koj/dot_general | solution.py:125
  281.0 2.6 pad_maximum_fusion.1
  283.6 9.1 copy.32
  292.7 8.8 reshape.57
  301.5 5.6 all-to-all-start.1
  307.4 35.5 %fusion.19 = f32[64,256,512]{2,0,1:T(8,128)} fusion(bf16[64,64]{1,0:T(8,128)(2,1)S(1)} %copy-done, bf16[8,8,256,512]{3,2,1,0:T(8,128)(2,1)} %bitcast.146), kind=kOutput, calls=%fused_computation.21 | convolution fusion | flops 1073741824 | bytes 50339840 | tf_op jit(solution)/shard_map/io,in->on/dot_general | solution.py:131
  342.9 11.4 %all-to-all-done.1 = f32[2,1,524288]{2,1,0:T(1,128)} async-done(((f32[2,1,524288]{2,1,0:T(1,128)}), f32[2,1,524288]{2,1,0:T(1,128)}, u32[]{:S(2)}, u32[]{:S(2)}) %all-to-all-start.1) | async-done | bytes 4194336 | tf_op jit(solution)/shard_map/all_to_all | solution.py:88
  354.8 16.6 %reduce = f32[2,524288]{1,0:T(2,128)} reduce(f32[2,1,524288]{2,1,0:T(1,128)} %all-to-all-done.1, f32[]{:T(128)} %broadcast.199), dimensions={1}, to_apply=%all_to_all.36.reduce_sub_computation | reduce | bytes 8388612 | tf_op jit(solution)/shard_map/all_to_all | solution.py:88
  371.4 10.1 %reshape.58 = f32[512,2,16,64]{3,2,1,0:T(8,128)} reshape(f32[2,524288]{1,0:T(2,128)} %reduce) | data formatting | bytes 8388608
  381.5 8.7 copy.33
  390.2 56.1 %fusion.10 = f32[64,256,512]{2,1,0:T(8,128)} fusion(f32[64,256,512]{2,0,1:T(8,128)} %fusion.19, f32[64]{0:T(128)S(1)} %copy-done.14, f32[64,256,64]{1,2,0:T(8,128)} %bitcast.149, f32[32,512]{1,0:T(8,128)S(1)} %get-tuple-element.21, f32[32,512]{1,0:T(8,128)S(1)} %get-tuple-element.22), kind=kOutput, calls=%fused_computation.12 | convolution fusion | flops 6467649536 | bytes 71434496 | tf_op jit(solution)/shard_map/dot_general | solution.py:90
  446.3 57.3 %fusion.7 = f32[64,256,2,32]{1,3,2,0:T(8,128)S(1)} fusion(f32[2,32,512,1]{2,1,0,3:T(8,128)S(1)} %bitcast.162, f32[64,256,512]{2,1,0:T(8,128)} %fusion.10, bf16[1,64,256,512]{3,2,1,0:T(8,128)(2,1)} %param.8), kind=kOutput, calls=%fused_computation.9 | convolution fusion | flops 6601834496 | bytes 54657024 | tf_op jit(solution)/shard_map/dot_general | solution.py:69
  503.6 5.2 copy.38
  508.8 5.6 all-to-all-start.2
  515.0 47.9 %all-to-all-done.2 = f32[64,256,2,32]{1,2,0,3:T(2,128)} async-done(((f32[64,256,2,32]{1,2,0,3:T(2,128)}), f32[64,256,2,32]{1,2,0,3:T(2,128)}, u32[]{:S(2)}, u32[]{:S(2)}) %all-to-all-start.2) | async-done | bytes 4194336 | tf_op jit(solution)/shard_map/all_to_all | solution.py:76
  562.9 7.4 copy.67
  570.3 6.7 reshape.42
  577.0 6.1 fusion.48
  583.1 6.1 fusion.54
  590.1 11.3 %multiply_add_fusion.1 = (f32[16,32,64,64]{3,2,1,0:T(8,128)S(1)}, f32[16,32,64,64]{3,2,1,0:T(8,128)}) fusion(f32[16,32,64]{2,1,0:T(8,128)S(1)} %copy.42, f32[16,32,64]{2,1,0:T(8,128)S(1)} %copy.41, f32[16,32,64]{2,1,0:T(8,128)S(1)} %copy.40, f32[16,32,64]{2,1,0:T(8,128)S(1)} %copy.37), kind=kLoop, calls=%fused_computation.27 | loop fusion | flops 12582912 | bytes 17301504 | tf_op jit(solution)/shard_map/add | solution.py:143
  601.3 13.1 %pad_maximum_fusion = f32[16,32,64,128]{3,2,1,0:T(8,128)} fusion(f32[16,32,64,64]{3,2,1,0:T(8,128)} %get-tuple-element.12, f32[16,32,64,64]{3,2,1,0:T(8,128)S(1)} %get-tuple-element.11), kind=kLoop, calls=%fused_computation.24 | loop fusion | flops 4194304 | bytes 33554432 | tf_op jit(solution)/shard_map/concatenate | solution.py:150
  616.4 22.2 %fusion.28 = bf16[1,64,256,512]{3,2,1,0:T(8,128)(2,1)} fusion(f32[64,256,512]{2,1,0:T(8,128)} %fusion.10), kind=kLoop, calls=%fused_computation.33 | loop fusion | flops 75497472 | bytes 50331648 | tf_op jit(solution)/shard_map/broadcast_in_dim | solution.py:138
  638.6 272.3 %all-reduce.3.cloned.1.call-done = f32[16,32,64,128]{3,2,1,0:T(8,128)} async-done(((f32[16,32,64,128]{3,2,1,0:T(8,128)}), f32[16,32,64,128]{3,2,1,0:T(8,128)}) %all-reduce.3.cloned.1.call-update) | async-done | bytes 16777232
  910.9 3.3 divide_subtract_fusion
  (91 shorter events, 44.7 us)
Async XLA Ops:
  7.2 300.2 %copy-start = (bf16[64,64]{1,0:T(8,128)(2,1)S(1)}, bf16[64,64]{1,0:T(8,128)(2,1)}, u32[]{:S(2)}) copy-start(bf16[64,64]{1,0:T(8,128)(2,1)} %param.12) | copy-start | bytes 24580
  7.2 18.3 %collective-permute-start = (f32[16,2,64,128]{3,2,1,0:T(8,128)}, f32[16,2,64,128]{3,2,1,0:T(8,128)S(1)}, u32[]{:S(2)}, u32[]{:S(2)}) collective-permute-start(f32[16,2,64,128]{3,2,1,0:T(8,128)} %param.9), channel_id=1, source_target_pairs={{0,2},{2,4},{4,6},{6,8},{8,10},{10,12},{12,14},{14,16},{16,18},{18... | collective-permute-start | bytes 3145736 | tf_op jit(solution)/shard_map/ppermute | solution.py:113
  7.7 25.9 %collective-permute-start.1 = (f32[16,2,64,128]{3,2,1,0:T(8,128)}, f32[16,2,64,128]{3,2,1,0:T(8,128)S(1)}, u32[]{:S(2)}, u32[]{:S(2)}) collective-permute-start(f32[16,2,64,128]{3,2,1,0:T(8,128)} %param.9), channel_id=1, source_target_pairs={{0,30},{2,0},{4,2},{6,4},{8,6},{10,8},{12,10},{14,12},{16,14},{18,... | collective-permute-start | bytes 3145736 | tf_op jit(solution)/shard_map/ppermute | solution.py:118
  25.5 17.0 %copy-start.6 = (f32[16,2,64,128]{3,2,1,0:T(8,128)}, f32[16,2,64,128]{3,2,1,0:T(8,128)S(1)}, u32[]{:S(2)}) copy-start(f32[16,2,64,128]{3,2,1,0:T(8,128)S(1)} %collective-permute-done) | copy-start | bytes 3145732
  25.5 17.0 %collective-permute-start.2 = (f32[16,2,64,128]{3,2,1,0:T(8,128)S(1)}, f32[16,2,64,128]{3,2,1,0:T(8,128)S(1)}, u32[]{:S(2)}, u32[]{:S(2)}) collective-permute-start(f32[16,2,64,128]{3,2,1,0:T(8,128)S(1)} %collective-permute-done), channel_id=1, source_target_pairs={{0,2},{2,4},{4,6},{6,8},{8,10},{10,12},{12,14},{14,16},{16,18},{18... | collective-permute-start | bytes 3145736 | tf_op jit(solution)/shard_map/ppermute | solution.py:113
  33.6 49.9 %copy-start.8 = (f32[16,2,64,128]{3,2,1,0:T(8,128)}, f32[16,2,64,128]{3,2,1,0:T(8,128)S(1)}, u32[]{:S(2)}) copy-start(f32[16,2,64,128]{3,2,1,0:T(8,128)S(1)} %collective-permute-done.1) | copy-start | bytes 3145732
  33.6 25.0 %collective-permute-start.3 = (f32[16,2,64,128]{3,2,1,0:T(8,128)S(1)}, f32[16,2,64,128]{3,2,1,0:T(8,128)}, u32[]{:S(2)}, u32[]{:S(2)}) collective-permute-start(f32[16,2,64,128]{3,2,1,0:T(8,128)S(1)} %collective-permute-done.1), channel_id=1, source_target_pairs={{0,30},{2,0},{4,2},{6,4},{8,6},{10,8},{12,10},{14,12},{16,14},{18,... | collective-permute-start | bytes 3145736 | tf_op jit(solution)/shard_map/ppermute | solution.py:118
  42.5 19.5 %collective-permute-start.4 = (f32[16,2,64,128]{3,2,1,0:T(8,128)S(1)}, f32[16,2,64,128]{3,2,1,0:T(8,128)}, u32[]{:S(2)}, u32[]{:S(2)}) collective-permute-start(f32[16,2,64,128]{3,2,1,0:T(8,128)S(1)} %collective-permute-done.2), channel_id=1, source_target_pairs={{0,2},{2,4},{4,6},{6,8},{8,10},{10,12},{12,14},{14,16},{16,18},{18... | collective-permute-start | bytes 3145736 | tf_op jit(solution)/shard_map/ppermute | solution.py:113
  58.6 52.3 %collective-permute-start.5 = (f32[16,2,64,128]{3,2,1,0:T(8,128)}, f32[16,2,64,128]{3,2,1,0:T(8,128)}, u32[]{:S(2)}, u32[]{:S(2)}) collective-permute-start(f32[16,2,64,128]{3,2,1,0:T(8,128)} %collective-permute-done.3), channel_id=1, source_target_pairs={{0,30},{2,0},{4,2},{6,4},{8,6},{10,8},{12,10},{14,12},{16,14},{18,... | collective-permute-start | bytes 3145736 | tf_op jit(solution)/shard_map/ppermute | solution.py:118
  62.0 49.0 %collective-permute-start.6 = (f32[16,2,64,128]{3,2,1,0:T(8,128)}, f32[16,2,64,128]{3,2,1,0:T(8,128)S(1)}, u32[]{:S(2)}, u32[]{:S(2)}) collective-permute-start(f32[16,2,64,128]{3,2,1,0:T(8,128)} %collective-permute-done.4), channel_id=1, source_target_pairs={{0,2},{2,4},{4,6},{6,8},{8,10},{10,12},{12,14},{14,16},{16,18},{18... | collective-permute-start | bytes 3145736 | tf_op jit(solution)/shard_map/ppermute | solution.py:113
  102.9 19.0 %copy-start.2 = (f32[16,2,64,128]{3,2,1,0:T(8,128)S(1)}, f32[16,2,64,128]{3,2,1,0:T(8,128)}, u32[]{:S(2)}) copy-start(f32[16,2,64,128]{3,2,1,0:T(8,128)} %param.9) | copy-start | bytes 3145732
  105.3 52.7 %all-to-all-start = ((f32[64,256,2,32]{1,0,2,3:T(8,128)}), f32[64,256,2,32]{1,0,2,3:T(8,128)}, u32[]{:S(2)}, u32[]{:S(2)}) async-start(f32[64,256,2,32]{1,0,2,3:T(8,128)} %copy.30), calls=%async_computation | async-start | bytes 8388608 | tf_op jit(solution)/shard_map/all_to_all | solution.py:76
  110.9 12.7 %collective-permute-start.7 = (f32[16,2,64,128]{3,2,1,0:T(8,128)}, f32[16,2,64,128]{3,2,1,0:T(8,128)}, u32[]{:S(2)}, u32[]{:S(2)}) collective-permute-start(f32[16,2,64,128]{3,2,1,0:T(8,128)} %collective-permute-done.5), channel_id=1, source_target_pairs={{0,30},{2,0},{4,2},{6,4},{8,6},{10,8},{12,10},{14,12},{16,14},{18,... | collective-permute-start | bytes 3145736 | tf_op jit(solution)/shard_map/ppermute | solution.py:118
  111.0 17.3 %collective-permute-start.8 = (f32[16,2,64,128]{3,2,1,0:T(8,128)S(1)}, f32[16,2,64,128]{3,2,1,0:T(8,128)}, u32[]{:S(2)}, u32[]{:S(2)}) collective-permute-start(f32[16,2,64,128]{3,2,1,0:T(8,128)S(1)} %collective-permute-done.6), channel_id=1, source_target_pairs={{0,2},{2,4},{4,6},{6,8},{8,10},{10,12},{12,14},{14,16},{16,18},{18... | collective-permute-start | bytes 3145736 | tf_op jit(solution)/shard_map/ppermute | solution.py:113
  113.7 33.7 %copy-start.7 = (f32[16,2,64,128]{3,2,1,0:T(8,128)S(1)}, f32[16,2,64,128]{3,2,1,0:T(8,128)}, u32[]{:S(2)}) copy-start(f32[16,2,64,128]{3,2,1,0:T(8,128)} %copy-done.6) | copy-start | bytes 3145732
  113.7 34.8 %copy-start.9 = (f32[16,2,64,128]{3,2,1,0:T(8,128)S(1)}, f32[16,2,64,128]{3,2,1,0:T(8,128)}, u32[]{:S(2)}) copy-start(f32[16,2,64,128]{3,2,1,0:T(8,128)} %copy-done.8) | copy-start | bytes 3145732
  123.6 60.6 %collective-permute-start.9 = (f32[16,2,64,128]{3,2,1,0:T(8,128)}, f32[16,2,64,128]{3,2,1,0:T(8,128)}, u32[]{:S(2)}, u32[]{:S(2)}) collective-permute-start(f32[16,2,64,128]{3,2,1,0:T(8,128)} %collective-permute-done.7), channel_id=1, source_target_pairs={{0,30},{2,0},{4,2},{6,4},{8,6},{10,8},{12,10},{14,12},{16,14},{18,... | collective-permute-start | bytes 3145736 | tf_op jit(solution)/shard_map/ppermute | solution.py:118
  128.3 56.0 %collective-permute-start.10 = (f32[16,2,64,128]{3,2,1,0:T(8,128)}, f32[16,2,64,128]{3,2,1,0:T(8,128)}, u32[]{:S(2)}, u32[]{:S(2)}) collective-permute-start(f32[16,2,64,128]{3,2,1,0:T(8,128)} %collective-permute-done.8), channel_id=1, source_target_pairs={{0,2},{2,4},{4,6},{6,8},{8,10},{10,12},{12,14},{14,16},{16,18},{18... | collective-permute-start | bytes 3145736 | tf_op jit(solution)/shard_map/ppermute | solution.py:113
  147.4 38.6 %copy-start.12 = (s32[32]{0:T(128)}, s32[32]{0:T(128)S(1)}, u32[]{:S(2)}) copy-start(s32[32]{0:T(128)S(1)} %pad_add_fusion) | copy-start | bytes 388
  184.2 12.7 %collective-permute-start.11 = (f32[16,2,64,128]{3,2,1,0:T(8,128)}, f32[16,2,64,128]{3,2,1,0:T(8,128)}, u32[]{:S(2)}, u32[]{:S(2)}) collective-permute-start(f32[16,2,64,128]{3,2,1,0:T(8,128)} %collective-permute-done.9), channel_id=1, source_target_pairs={{0,30},{2,0},{4,2},{6,4},{8,6},{10,8},{12,10},{14,12},{16,14},{18,... | collective-permute-start | bytes 3145736 | tf_op jit(solution)/shard_map/ppermute | solution.py:118
  184.3 19.6 %collective-permute-start.12 = (f32[16,2,64,128]{3,2,1,0:T(8,128)}, f32[16,2,64,128]{3,2,1,0:T(8,128)}, u32[]{:S(2)}, u32[]{:S(2)}) collective-permute-start(f32[16,2,64,128]{3,2,1,0:T(8,128)} %collective-permute-done.10), channel_id=1, source_target_pairs={{0,2},{2,4},{4,6},{6,8},{8,10},{10,12},{12,14},{14,16},{16,18},{18... | collective-permute-start | bytes 3145736 | tf_op jit(solution)/shard_map/ppermute | solution.py:113
  196.9 38.9 %collective-permute-start.13 = (f32[16,2,64,128]{3,2,1,0:T(8,128)}, f32[16,2,64,128]{3,2,1,0:T(8,128)S(1)}, u32[]{:S(2)}, u32[]{:S(2)}) collective-permute-start(f32[16,2,64,128]{3,2,1,0:T(8,128)} %collective-permute-done.11), channel_id=1, source_target_pairs={{0,30},{2,0},{4,2},{6,4},{8,6},{10,8},{12,10},{14,12},{16,14},{18,... | collective-permute-start | bytes 3145736 | tf_op jit(solution)/shard_map/ppermute | solution.py:118
  204.0 32.9 %collective-permute-start.14 = (f32[16,2,64,128]{3,2,1,0:T(8,128)}, f32[16,2,64,128]{3,2,1,0:T(8,128)S(1)}, u32[]{:S(2)}, u32[]{:S(2)}) collective-permute-start(f32[16,2,64,128]{3,2,1,0:T(8,128)} %collective-permute-done.12), channel_id=1, source_target_pairs={{0,2},{2,4},{4,6},{6,8},{8,10},{10,12},{12,14},{14,16},{16,18},{18... | collective-permute-start | bytes 3145736 | tf_op jit(solution)/shard_map/ppermute | solution.py:113
  254.8 17.0 %copy-start.13 = (s32[32]{0:T(128)S(1)}, s32[32]{0:T(128)}, u32[]{:S(2)}) copy-start(s32[32]{0:T(128)} %copy-done.12) | copy-start | bytes 388
  301.5 52.9 %all-to-all-start.1 = ((f32[2,1,524288]{2,1,0:T(1,128)}), f32[2,1,524288]{2,1,0:T(1,128)}, u32[]{:S(2)}, u32[]{:S(2)}) async-start(f32[2,1,524288]{2,1,0:T(1,128)} %reshape.57), calls=%async_computation.1 | async-start | bytes 8388608 | tf_op jit(solution)/shard_map/all_to_all | solution.py:88
  354.8 35.4 %copy-start.14 = (f32[64]{0:T(128)S(1)}, f32[64]{0:T(128)}, u32[]{:S(2)}) copy-start(f32[64]{0:T(128)} %param.13) | copy-start | bytes 772
  503.6 10.9 %copy-start.5 = (f32[16,32,64]{1,0,2:T(8,128)S(1)}, f32[16,32,64]{1,0,2:T(8,128)}, u32[]{:S(2)}) copy-start(f32[16,32,64]{1,0,2:T(8,128)} %get-tuple-element.13) | copy-start | bytes 393220
  503.6 11.2 %copy-start.4 = (f32[16,32,64]{1,0,2:T(8,128)S(1)}, f32[16,32,64]{1,0,2:T(8,128)}, u32[]{:S(2)}) copy-start(f32[16,32,64]{1,0,2:T(8,128)} %get-tuple-element.16) | copy-start | bytes 393220
  508.8 54.1 %all-to-all-start.2 = ((f32[64,256,2,32]{1,2,0,3:T(2,128)}), f32[64,256,2,32]{1,2,0,3:T(2,128)}, u32[]{:S(2)}, u32[]{:S(2)}) async-start(f32[64,256,2,32]{1,2,0,3:T(2,128)} %copy.38), calls=%async_computation.2 | async-start | bytes 8388608 | tf_op jit(solution)/shard_map/all_to_all | solution.py:76
  514.4 396.5 %all-reduce.3.cloned.1.call-start = ((), (), s32[]{:S(2)}) async-start(), calls=%async_computation.3 | async-start | bytes 33554432
  614.5 0.7 copy-start.15
  615.7 298.6 %copy-start.1 = (bf16[64,64]{1,0:T(8,128)(2,1)S(1)}, bf16[64,64]{1,0:T(8,128)(2,1)}, u32[]{:S(2)}) copy-start(bf16[64,64]{1,0:T(8,128)(2,1)} %param.12) | copy-start | bytes 24580
  616.4 294.5 %copy-start.3 = (f32[16,2,64,128]{3,2,1,0:T(8,128)S(1)}, f32[16,2,64,128]{3,2,1,0:T(8,128)}, u32[]{:S(2)}) copy-start(f32[16,2,64,128]{3,2,1,0:T(8,128)} %param.9) | copy-start | bytes 3145732
  616.4 294.5 %copy-start.10 = (f32[16,2,64,128]{3,2,1,0:T(8,128)S(1)}, f32[16,2,64,128]{3,2,1,0:T(8,128)}, u32[]{:S(2)}) copy-start(f32[16,2,64,128]{3,2,1,0:T(8,128)} %param.10) | copy-start | bytes 3145732
  616.4 294.5 %copy-start.11 = (f32[16,2,64,128]{3,2,1,0:T(8,128)S(1)}, f32[16,2,64,128]{3,2,1,0:T(8,128)}, u32[]{:S(2)}) copy-start(f32[16,2,64,128]{3,2,1,0:T(8,128)} %param.11) | copy-start | bytes 3145732
Sparse Core Ops, SparseCore 0:
  614.6 296.2 all-reduce.2
